TPU v7x, 32 devices: a whole 2x2x4 slice. The times are simulated.
32 devices in a mesh: groups: 2 (over x), fsdp: 16 (over z, y, core).
Axes of the slice: x: 2, y: 2, z: 4, core: 2. Of those that a mesh axis runs over, the one named last changes fastest.
Arguments:
- hidden: bfloat16 [4096, 8192], P(('groups', 'fsdp')), parts along dimension 0, may hold values from -6 to 6
- output_gradient: bfloat16 [4096, 512], P(('groups', 'fsdp')), parts along dimension 0, may hold values from -6 to 6
- frozen_value_weight: bfloat16 [8192, 512], P('fsdp'), may hold values from -0.0625 to 0.0625
- adapter_down_maps: bfloat16 [16, 8192, 32], P('fsdp'), may hold values from -0.0625 to 0.0625
- adapter_up_maps: bfloat16 [16, 32, 512], P('fsdp'), may hold values from -1 to 1
- owner: int32 [16], replicated, may hold values from 0 to 15, each once
- token_block_tenant: int32 [32, 1], P(('groups', 'fsdp')), parts along dimension 0, may hold values from 0 to 15
Outputs:
- values: bfloat16 [4096, 512], P(('groups', 'fsdp')), parts along dimension 0
- grad_hidden: bfloat16 [4096, 8192], P(('groups', 'fsdp')), parts along dimension 0
- grad_down: float32 [32, 8192, 32], P(('groups', 'fsdp')), parts along dimension 0
- up_map_gradient: float32 [32, 32, 512], P(('groups', 'fsdp')), parts along dimension 0
There are 2 independent parts, one for each index of `groups`. A program takes and returns all parts, laid end to end along the dimension named above; an argument that names none is the same for every part. Nothing has to cross between parts.
Inputs may be any that keep to these rules, and one draw needn't show every extreme that they name: `owner`: each tenant has exactly one slot, each slot one tenant.
All inputs are finite; a program needn't handle non-finite values.
Results may differ from a plain program's by a relative error of at most 0.0055.
Values may be sent and summed in bfloat16 or wider, within the bound.
A program may use at most 128 MiB of HBM per device.

v0:
```python
import jax
import jax.numpy as jnp
from jax import lax
from jax.sharding import PartitionSpec as P

adapter_scale = 2.0


def per_device(
    hidden,
    output_gradient,
    frozen_value_weight,
    adapter_down_maps,
    adapter_up_maps,
    owner,
    token_block_tenant,
):
    shards = lax.axis_size("fsdp")
    token_rows, model_width = hidden.shape
    local_blocks = token_block_tenant.shape[0]
    blk_rows = token_rows // local_blocks
    tenants = owner.shape[0]
    reduced_rank_rows = adapter_down_maps.shape[2]
    output_list = output_gradient.shape[1]
    slice_width = model_width // shards
    tenant_ids = jnp.arange(tenants, dtype=jnp.int32)
    slot_ids = jnp.arange(shards, dtype=jnp.int32)

    def slot_of(tenant_col):
        matches = tenant_col[:, None] == tenant_ids[None, :]
        return jnp.sum(jnp.where(matches, owner[None, :], 0), axis=1)

    all_tenants = lax.all_gather(token_block_tenant, "fsdp", axis=0, tiled=True)
    local_slots = slot_of(token_block_tenant[:, 0])
    all_slots = slot_of(all_tenants[:, 0])
    all_blocks = all_slots.shape[0]
    all_onehot = (all_slots[:, None] == slot_ids[None, :]).astype(jnp.float32)
    local_onehot = (local_slots[:, None] == slot_ids[None, :]).astype(jnp.float32)
    down_map_pieces = lax.all_to_all(
        adapter_down_maps, "fsdp", split_axis=1, concat_axis=0, tiled=True
    )
    token_cols = lax.all_to_all(hidden, "fsdp", split_axis=1, concat_axis=0, tiled=True)
    down_map_blocks = down_map_pieces[all_slots]
    row_count = token_rows * lax.axis_size("fsdp")
    block_count = row_count // blk_rows
    block_of_rows = token_cols
    block_of_rows = block_of_rows.reshape(block_count, blk_rows, slice_width)
    partial_terms = jnp.einsum(
        "vxh,vht->vxt", block_of_rows, down_map_blocks, preferred_element_type=jnp.float32
    )
    reduced_projection = lax.psum_scatter(
        partial_terms.reshape(row_count, reduced_rank_rows), "fsdp", scatter_dimension=0, tiled=True
    ).astype(jnp.bfloat16)
    every_up_map = lax.all_gather(adapter_up_maps, "fsdp", axis=0, tiled=True)
    up_local = every_up_map[local_slots]
    weights_full = lax.all_gather(frozen_value_weight, "fsdp", axis=0, tiled=True)
    low_blocks = reduced_projection.reshape(local_blocks, blk_rows, reduced_rank_rows)
    adapter_output = jnp.einsum(
        "bkr,brv->bkv", low_blocks, up_local, preferred_element_type=jnp.float32
    )
    frozen_output = jnp.dot(hidden, weights_full, preferred_element_type=jnp.float32)
    values = (
        frozen_output + adapter_scale * adapter_output.reshape(token_rows, output_list)
    ).astype(jnp.bfloat16)
    gradient_block_list = output_gradient.reshape(local_blocks, blk_rows, output_list)
    backward_low_rank = adapter_scale * jnp.einsum(
        "jui,jti->jut", gradient_block_list, up_local, preferred_element_type=jnp.float32
    )
    backward_low_rank = backward_low_rank.astype(jnp.bfloat16).reshape(
        token_rows, reduced_rank_rows
    )
    block_up_map = jnp.einsum(
        "bkr,bkv->brv", low_blocks, gradient_block_list, preferred_element_type=jnp.float32
    )
    slot_up_map = adapter_scale * jnp.einsum(
        "bs,brv->srv", local_onehot, block_up_map, precision=lax.Precision.HIGHEST
    )
    up_map_gradient = lax.psum_scatter(slot_up_map, "fsdp", scatter_dimension=0, tiled=True)
    back_all = lax.all_gather(backward_low_rank, "fsdp", axis=0, tiled=True)
    backward_block_list = back_all.reshape(all_blocks, blk_rows, reduced_rank_rows)
    side_cols = jnp.einsum(
        "jsn,jwn->jsw", backward_block_list, down_map_blocks, preferred_element_type=jnp.float32
    )
    side_cols = side_cols.astype(jnp.bfloat16).reshape(all_blocks * blk_rows, slice_width)
    adapter_gradient = lax.all_to_all(side_cols, "fsdp", split_axis=0, concat_axis=1, tiled=True)
    token_block_list = token_cols.reshape(all_blocks, blk_rows, slice_width)
    block_down_map = jnp.einsum(
        "fmy,fmo->fyo", token_block_list, backward_block_list, preferred_element_type=jnp.float32
    )
    slot_down = jnp.einsum(
        "bs,bdr->sdr", all_onehot, block_down_map, precision=lax.Precision.HIGHEST
    )
    base_grad = jnp.einsum(
        "kv,dv->kd", output_gradient, weights_full, preferred_element_type=jnp.float32
    )
    grad_hidden = (base_grad + adapter_gradient.astype(jnp.float32)).astype(jnp.bfloat16)
    grad_down = lax.all_to_all(slot_down, "fsdp", split_axis=0, concat_axis=1, tiled=True)
    return (values, grad_hidden, grad_down, up_map_gradient)


def solution(mesh):
    return jax.shard_map(
        per_device,
        mesh=mesh,
        in_specs=(
            P(("groups", "fsdp"), None),
            P(("groups", "fsdp"), None),
            P("fsdp", None),
            P("fsdp", None, None),
            P("fsdp", None, None),
            P(),
            P(("groups", "fsdp"), None),
        ),
        out_specs=(
            P(("groups", "fsdp"), None),
            P(("groups", "fsdp"), None),
            P(("groups", "fsdp"), None, None),
            P(("groups", "fsdp"), None, None),
        ),
        check_vma=False,
    )
```

profile of v0, /device:TPU:0, one launch (start us, length us, event | category | flops | bytes accessed | tf_op | source)
XLA Modules:
  0.0 401.2 jit_solution(12266302114022567275)
XLA Ops:
  7.2 8.6 %copy.49 = bf16[1,8192,32]{2,0,1:T(2,128)(2,1)} copy(bf16[1,8192,32]{1,2,0:T(8,128)(2,1)} %param.10) | data formatting | bytes 1048576 | tf_op args[3]
  16.3 46.5 %reduce.2 = bf16[8192,32]{1,0:T(8,128)(2,1)} reduce(bf16[8192,1,32]{2,1,0:T(2,128)(2,1)} %bitcast.73, bf16[]{:T(256)} %broadcast.65), dimensions={1}, to_apply=%bitcast.54.reduce_sub_computation | reduce | bytes 1048578
  62.9 4.7 %reshape.132 = bf16[16,2,8192]{2,1,0:T(2,128)(2,1)} reshape(bf16[8192,32]{1,0:T(8,128)(2,1)} %reduce.2) | data formatting | bytes 1048576
  67.5 7.4 %all-to-all-start = ((bf16[16,2,8192]{2,1,0:T(2,128)(2,1)}), bf16[16,2,8192]{2,1,0:T(2,128)(2,1)S(1)}, u32[]{:S(2)}, u32[]{:S(2)}) async-start(bf16[16,2,8192]{2,1,0:T(2,128)(2,1)} %reshape.132), calls=%async_computation | async-start | bytes 1048576 | tf_op jit(solution)/shard_map/all_to_all | solution.py:39
  74.9 2.4 copy.52
  77.4 3.9 copy.53
  81.3 8.1 %all-to-all-done = bf16[16,2,8192]{2,1,0:T(2,128)(2,1)S(1)} async-done(((bf16[16,2,8192]{2,1,0:T(2,128)(2,1)}), bf16[16,2,8192]{2,1,0:T(2,128)(2,1)S(1)}, u32[]{:S(2)}, u32[]{:S(2)}) %all-to-all-start) | async-done | bytes 524320 | tf_op jit(solution)/shard_map/all_to_all | solution.py:39
  89.4 4.1 %all-to-all-start.1 = ((bf16[128,16,512]{2,0,1:T(8,128)(2,1)}), bf16[128,16,512]{2,0,1:T(8,128)(2,1)S(1)}, u32[]{:S(2)}, u32[]{:S(2)}) async-start(bf16[128,16,512]{2,0,1:T(8,128)(2,1)} %copy.53), calls=%async_computation.1 | async-start | bytes 4194304 | tf_op jit(solution)/shard_map/all_to_all | solution.py:42
  95.5 47.3 %all-reduce = s32[16]{0:T(128)S(1)} all-reduce(s32[16]{0:T(128)S(1)} %bitcast_dynamic-update-slice_fusion), channel_id=1, replica_groups=mesh['groups'=2,'fsdp'=16] {'fsdp'}, use_global_device_ids=true, to_apply=%add | all-reduce | flops 16 | bytes 128
  143.0 7.1 %reshape.133 = bf16[8192,1,32]{2,1,0:T(2,128)(2,1)} reshape(bf16[16,2,8192]{2,1,0:T(2,128)(2,1)S(1)} %all-to-all-done) | data formatting | bytes 1048576
  150.0 8.0 %copy.50 = bf16[1,8192,32]{1,2,0:T(8,128)(2,1)S(1)} copy(bf16[1,8192,32]{2,0,1:T(2,128)(2,1)} %bitcast.74) | data formatting | bytes 1048576 | tf_op jit(solution)/shard_map/all_to_all | solution.py:39
  164.0 20.8 %all_gather.14 = bf16[16,32,512]{2,1,0:T(8,128)(2,1)S(1)} all-gather(bf16[1,32,512]{2,1,0:T(8,128)(2,1)S(1)} %copy-done.7), channel_id=1, replica_groups=mesh['groups'=2,'fsdp'=16] {'fsdp'}, dimensions={0}, use_global_device_ids=true | all-gather | bytes 557056 | tf_op jit(solution)/shard_map/all_gather | solution.py:54
  185.8 17.8 %all_gather.15 = bf16[2048,32]{0,1:T(8,128)(2,1)S(1)} all-gather(bf16[128,32]{0,1:T(8,128)(2,1)S(1)} %fusion.14), channel_id=1, replica_groups=mesh['groups'=2,'fsdp'=16] {'fsdp'}, dimensions={0}, use_global_device_ids=true | all-gather | bytes 139264 | tf_op jit(solution)/shard_map/all_gather | solution.py:79
  205.6 4.6 %all-to-all-start.2 = ((bf16[16,128,512]{2,1,0:T(8,128)(2,1)}), bf16[16,128,512]{2,1,0:T(8,128)(2,1)}, u32[]{:S(2)}, u32[]{:S(2)}) async-start(bf16[16,128,512]{2,1,0:T(8,128)(2,1)} %convolution_convert_fusion), calls=%async_computation.3 | async-start | bytes 4194304 | tf_op jit(solution)/shard_map/all_to_all | solution.py:85
  213.5 53.9 %all-to-all-done.2 = bf16[16,128,512]{2,1,0:T(8,128)(2,1)} async-done(((bf16[16,128,512]{2,1,0:T(8,128)(2,1)}), bf16[16,128,512]{2,1,0:T(8,128)(2,1)}, u32[]{:S(2)}, u32[]{:S(2)}) %all-to-all-start.2) | async-done | bytes 2097184 | tf_op jit(solution)/shard_map/all_to_all | solution.py:85
  267.4 18.1 %all-to-all-start.3 = ((f32[16,512,32]{1,2,0:T(8,128)}), f32[16,512,32]{1,2,0:T(8,128)S(1)}, u32[]{:S(2)}, u32[]{:S(2)}) async-start(f32[16,512,32]{1,2,0:T(8,128)} %copy.59), calls=%async_computation.4 | async-start | bytes 2097152 | tf_op jit(solution)/shard_map/all_to_all | solution.py:97
  290.5 2.6 copy.63
  293.1 30.9 %all-to-all-done.3 = f32[16,512,32]{1,2,0:T(8,128)S(1)} async-done(((f32[16,512,32]{1,2,0:T(8,128)}), f32[16,512,32]{1,2,0:T(8,128)S(1)}, u32[]{:S(2)}, u32[]{:S(2)}) %all-to-all-start.3) | async-done | bytes 1048608 | tf_op jit(solution)/shard_map/all_to_all | solution.py:97
  325.6 2.4 all_to_all.45
  328.0 5.3 %all-gather.2.cloned.1.call-done = bf16[8192,512]{1,0:T(8,128)(2,1)} async-done(((bf16[512,512]{1,0:T(8,128)(2,1)}), bf16[8192,512]{1,0:T(8,128)(2,1)}) %all-gather.2.cloned.1.call-update) | async-done | bytes 8388624 | tf_op jit(solution)/shard_map/all_gather | solution.py:56
  333.4 4.8 %fusion.35 = f32[128,512]{1,0:T(8,128)S(1)} fusion(bf16[128,8192]{1,0:T(8,128)(2,1)S(1)} %copy-done.4, bf16[8192,512]{1,0:T(8,128)(2,1)} %all-gather.2.cloned.1.call-done), kind=kOutput, calls=%fused_computation.46 | convolution fusion | flops 1073741824 | bytes 10747904 | tf_op jit(solution)/shard_map/dot_general | solution.py:61
  338.2 2.4 fusion.12
  340.5 4.2 %fusion = bf16[128,8192]{1,0:T(8,128)(2,1)} fusion(f32[128,8192]{1,0:T(8,128)S(1)} %bitcast.72, bf16[128,512]{1,0:T(8,128)(2,1)S(1)} %copy-done, bf16[8192,512]{1,0:T(8,128)(2,1)S(1)} %copy-done.1), kind=kOutput, calls=%fused_computation.2 | convolution fusion | flops 1075838976 | bytes 14811136 | tf_op jit(solution)/shard_map/kv,dv->kd/dot_general | solution.py:93
  344.7 50.0 %reduce-scatter.5.cloned.1.call-done = f32[1,32,512]{2,1,0:T(8,128)} async-done(((f32[16,32,512]{2,1,0:T(8,128)}), f32[1,32,512]{2,1,0:T(8,128)}) %reduce-scatter.5.cloned.1.call-update) | async-done | bytes 65552 | tf_op jit(solution)/shard_map/reduce_scatter | solution.py:78
  (51 shorter events, 18.7 us)
Async XLA Ops:
  7.2 178.5 %copy-start = (bf16[128,512]{1,0:T(8,128)(2,1)S(1)}, bf16[128,512]{1,0:T(8,128)(2,1)}, u32[]{:S(2)}) copy-start(bf16[128,512]{1,0:T(8,128)(2,1)} %param.8) | copy-start | bytes 393220
  62.9 12.1 %copy-start.3 = (bf16[128,8192]{1,0:T(8,128)(2,1)S(1)}, bf16[128,8192]{1,0:T(8,128)(2,1)}, u32[]{:S(2)}) copy-start(bf16[128,8192]{1,0:T(8,128)(2,1)} %param.7) | copy-start | bytes 6291460
  67.5 21.9 %all-to-all-start = ((bf16[16,2,8192]{2,1,0:T(2,128)(2,1)}), bf16[16,2,8192]{2,1,0:T(2,128)(2,1)S(1)}, u32[]{:S(2)}, u32[]{:S(2)}) async-start(bf16[16,2,8192]{2,1,0:T(2,128)(2,1)} %reshape.132), calls=%async_computation | async-start | bytes 1048576 | tf_op jit(solution)/shard_map/all_to_all | solution.py:39
  81.3 12.9 %copy-start.9 = (u32[32]{0:T(128)S(1)}, u32[32]{0:T(128)}, u32[]{:S(2)}) copy-start(u32[32]{0:T(128)} %constant.37) | copy-start | bytes 388
  81.3 61.5 %copy-start.8 = (s32[16]{0:T(128)S(1)}, s32[16]{0:T(128)}, u32[]{:S(2)}) copy-start(s32[16]{0:T(128)} %param.12) | copy-start | bytes 196
  89.4 69.7 %all-to-all-start.1 = ((bf16[128,16,512]{2,0,1:T(8,128)(2,1)}), bf16[128,16,512]{2,0,1:T(8,128)(2,1)S(1)}, u32[]{:S(2)}, u32[]{:S(2)}) async-start(bf16[128,16,512]{2,0,1:T(8,128)(2,1)} %copy.53), calls=%async_computation.1 | async-start | bytes 4194304 | tf_op jit(solution)/shard_map/all_to_all | solution.py:42
  93.5 192.8 %reduce-scatter.3.cloned.1.call-start = ((), (), s32[]{:S(2)}) async-start(), calls=%async_computation.7 | async-start | bytes 278528 | tf_op jit(solution)/shard_map/reduce_scatter | solution.py:51
  159.1 4.9 %copy-start.7 = (bf16[1,32,512]{2,1,0:T(8,128)(2,1)S(1)}, bf16[1,32,512]{2,1,0:T(8,128)(2,1)}, u32[]{:S(2)}) copy-start(bf16[1,32,512]{2,1,0:T(8,128)(2,1)} %param.11) | copy-start | bytes 98308
  160.6 172.7 %all-gather.2.cloned.1.call-start = ((), (), s32[]{:S(2)}) async-start(), calls=%async_computation.6 | async-start | bytes 8912896 | tf_op jit(solution)/shard_map/all_gather | solution.py:56
  184.8 0.8 copy-start.5
  205.6 61.8 %all-to-all-start.2 = ((bf16[16,128,512]{2,1,0:T(8,128)(2,1)}), bf16[16,128,512]{2,1,0:T(8,128)(2,1)}, u32[]{:S(2)}, u32[]{:S(2)}) async-start(bf16[16,128,512]{2,1,0:T(8,128)(2,1)} %convolution_convert_fusion), calls=%async_computation.3 | async-start | bytes 4194304 | tf_op jit(solution)/shard_map/all_to_all | solution.py:85
  267.4 56.6 %all-to-all-start.3 = ((f32[16,512,32]{1,2,0:T(8,128)}), f32[16,512,32]{1,2,0:T(8,128)S(1)}, u32[]{:S(2)}, u32[]{:S(2)}) async-start(f32[16,512,32]{1,2,0:T(8,128)} %copy.59), calls=%async_computation.4 | async-start | bytes 2097152 | tf_op jit(solution)/shard_map/all_to_all | solution.py:97
  285.5 109.2 %reduce-scatter.5.cloned.1.call-start = ((), (), s32[]{:S(2)}) async-start(), calls=%async_computation.8 | async-start | bytes 1114112 | tf_op jit(solution)/shard_map/reduce_scatter | solution.py:78
  293.1 40.2 %copy-start.4 = (bf16[128,8192]{1,0:T(8,128)(2,1)S(1)}, bf16[128,8192]{1,0:T(8,128)(2,1)}, u32[]{:S(2)}) copy-start(bf16[128,8192]{1,0:T(8,128)(2,1)} %param.7) | copy-start | bytes 6291460
  328.0 10.1 %copy-start.6 = (f32[128,32]{0,1:T(8,128)S(1)}, f32[128,32]{0,1:T(8,128)}, u32[]{:S(2)}) copy-start(f32[128,32]{0,1:T(8,128)} %reduce-scatter.3.cloned.1.call-done) | copy-start | bytes 49156
  333.4 7.2 %copy-start.1 = (bf16[8192,512]{1,0:T(8,128)(2,1)S(1)}, bf16[8192,512]{1,0:T(8,128)(2,1)}, u32[]{:S(2)}) copy-start(bf16[8192,512]{1,0:T(8,128)(2,1)} %all-gather.2.cloned.1.call-done) | copy-start | bytes 25165828
  333.4 7.2 %copy-start.2 = (f32[16,16,8,512]{3,2,0,1:T(8,128)S(1)}, f32[16,16,8,512]{3,2,0,1:T(8,128)}, u32[]{:S(2)}) copy-start(f32[16,16,8,512]{3,2,0,1:T(8,128)} %copy.63) | copy-start | bytes 12582916
Sparse Core Ops, SparseCore 0:
  160.8 54.4 reduce-scatter.2
  217.4 115.9 all-gather.1
  337.5 57.1 reduce-scatter.4
where the time goes:
time: 403 us; the launch traced here: 401 us
  waiting for transfers between devices  149 us (37%)
  blocking collectives  85.9 us (21%)
  other arithmetic  51.3 us (13%)
  local copies, waits for them, and re-layouts  47.2 us (12%)
  starting transfers between devices  34.3 us (9%)
  matrix products  16.8 us (4%)
  between operations  16.5 us (4%)
    all_to_all x1, waiting for transfers between devices, per_device(): lax.all_to_all(side_cols, 'fsdp', split_axis=0, concat_axis=1, tiled=True)  53.9 us
    reduce_scatter x1, waiting for transfers between devices, per_device(): lax.psum_scatter(slot_up_map, 'fsdp', scatter_dimension=0, tiled=True)  50 us
    unnamed x2, other arithmetic  48.7 us
    unnamed x1, blocking collectives  47.3 us
    all_to_all x1, waiting for transfers between devices, per_device(): lax.all_to_all(slot_down, 'fsdp', split_axis=0, concat_axis=1, tiled=True)  30.9 us
    unnamed x29, local copies, waits for them, and re-layouts  25.6 us
    all_gather x1, blocking collectives, per_device(): every_up_map = lax.all_gather(adapter_up_maps, 'fsdp', axis=0, tiled=True)  20.8 us
    all_to_all x1, starting transfers between devices, per_device(): lax.all_to_all(slot_down, 'fsdp', split_axis=0, concat_axis=1, tiled=True)  18.1 us
  transfers between devices with their start and end apart: 7, of which 5 were waited for; matrix products, arithmetic and copies ran while one was open for 13% of the time, Pallas kernels for 0%

commit v1 on v0

v1 whole, which is shorter than its diff:
```python
import functools

import jax
import jax.numpy as jnp
from jax import lax
from jax.experimental import pallas as pl
from jax.experimental.pallas import tpu as pltpu
from jax.sharding import PartitionSpec as P

MESH = pl.DeviceIdType.MESH
adapter_scale = 2.0
F32 = jnp.float32
BF16 = jnp.bfloat16


def dot(a, b, over):
    return lax.dot_general(a, b, ((over[:1], over[1:]), ((), ())), preferred_element_type=F32)


class Ring:
    def __init__(self, place, pool, buf, axis, shared):
        self.place, self.pool, self.buf, self.axis = place, pool, buf, axis
        length = buf.shape[axis]
        self.shared = shared
        self.length = length // 2 if shared else length
        self.start_at = place["side"] * self.length if shared else 0
        self.other_at = (1 - place["side"]) * self.length if shared else 0
        self.right, self.left, self.twin, self.near = {}, {}, {}, {}
        self.near_twin = {}

    def view(self, index, start, length):
        if self.axis == 1:
            return self.buf.at[index, pl.ds(pl.multiple_of(start, 16), length), :]
        return self.buf.at[index, :, pl.ds(pl.multiple_of(start, 128), length)]

    def send(self, index, start, length, to):
        ref = self.view(index, start, length)
        return self.pool(ref, to)

    def chip(self, offset):
        place = self.place
        return place["chip_at"](lax.rem(place["spot"] + offset + place["chips"], place["chips"]))

    def mine(self, offset):
        return self.chip(offset) * 2 + self.place["core"]

    def begin(self):
        place = self.place
        self.near[0] = [self.send(place["me"], 0, self.buf.shape[self.axis], place["near"])]
        self.right[1] = self.send(place["me"], self.start_at, self.length, place["right"])
        self.left[1] = self.send(place["me"], self.start_at, self.length, place["left"])

    def step(self, k):
        place, half = self.place, self.length // 2
        last = place["chips"] // 2
        from_left, from_right = self.mine(-k), self.mine(k)
        self.right[k].wait_recv()
        if k + 1 <= last:
            size = self.length if k + 1 < last else half
            self.right[k + 1] = self.send(from_left, self.start_at, size, place["right"])
        self.left[k].wait_recv()
        if k + 1 <= last:
            size = self.length if k + 1 < last else half
            self.left[k + 1] = self.send(
                from_right, self.start_at + self.length - size, size, place["left"]
            )
        got = [from_left, from_right] if k < last else [from_left]
        if self.shared:
            self.twin[k] = [self.send(i, self.start_at, self.length, place["twin"]) for i in got]
        self.near[k] = [self.send(i, self.start_at, self.length, place["near"]) for i in got]

    def cross(self, k):
        place, last = self.place, self.place["chips"] // 2
        got = [self.mine(-k), self.mine(k)] if k < last else [self.mine(-k)]
        self.near_twin[k] = []
        for i, copy in zip(got, self.twin[k]):
            copy.wait_recv()
            self.near_twin[k].append(self.send(i, self.other_at, self.length, place["near"]))

    def settle(self, k):
        for copy in self.near[k]:
            copy.wait_recv()
        for copy in self.near_twin.get(k, []):
            copy.wait_recv()


def copies_of(chips, shared):
    last = chips // 2
    got = 2 * last - 1
    return 1 + 2 * last + got * (3 if shared else 1)


def kernel(
    n, ring_of, staged,
    slot_ref, hidden, gradient, weight, down, up,
    values, grad_hidden, grad_down, grad_up, *rest,
):
    if staged:
        parts, w_all, d_all, u_all, t_all, back, stage, send_sems, recv_sems, local_sems = rest
    else:
        parts, w_all, d_all, u_all, t_all, back, send_sems, recv_sems, local_sems = rest
    me = lax.axis_index("fsdp")
    group = lax.axis_index("groups")
    chips, last = n // 2, n // 4
    core, chip = lax.rem(me, 2), me // 2
    chip_at, spot_of = ring_of
    spot = spot_of(chip)
    side = lax.rem(group, 2)

    def device(at):
        return (group, chip_at(lax.rem(spot + at + chips, chips)) * 2 + core)

    place = {
        "me": me, "core": core, "spot": spot, "side": side, "chips": chips, "chip_at": chip_at,
        "right": device(1), "left": device(-1),
        "near": (group, chip * 2 + 1 - core), "twin": (group + 1 - 2 * side, me),
    }
    local = [
        pltpu.make_async_copy(src, dst.at[me], local_sems.at[i])
        for i, (src, dst) in enumerate(((up, u_all), (down, d_all), (weight, w_all)))
    ]
    for copy in local:
        copy.start()

    barrier = pltpu.get_barrier_semaphore()
    for to in ("right", "left", "near", "twin"):
        pl.semaphore_signal(barrier, inc=1, device_id=place[to], device_id_type=MESH)
    pl.semaphore_wait(barrier, 4)

    sent = []

    def pool(ref, to):
        i = len(sent)
        copy = pltpu.make_async_remote_copy(
            src_ref=ref, dst_ref=ref, send_sem=send_sems.at[i], recv_sem=recv_sems.at[i],
            device_id=to, device_id_type=MESH,
        )
        copy.start()
        sent.append(copy)
        return copy

    ups = Ring(place, pool, u_all, 2, False)
    downs = Ring(place, pool, d_all, 2, True)
    weights = Ring(place, pool, w_all, 1, True)
    terms = Ring(place, pool, parts, 2, False)
    up_terms = Ring(place, pool, t_all, 2, False)

    local[0].wait()
    ups.begin()
    local[1].wait()
    downs.begin()
    for k in range(1, last + 1):
        ups.step(k)
        if k == 1:
            local[2].wait()
            weights.begin()
    for k in range(last + 1):
        ups.settle(k)

    rank, width = down.shape
    tile = 1024
    slot = slot_ref[0]
    up_slot = u_all[slot][:rank, :]
    back_low = (adapter_scale * dot(gradient[...], up_slot, (1, 1))).astype(BF16)
    back[...] = back_low
    back_turned = back_low.astype(F32).T.astype(BF16)
    mine = stage if staged else parts.at[me]

    @pl.loop(0, width // tile)
    def _(t):
        at = pl.ds(pl.multiple_of(t * tile, tile), tile)
        term = dot(back_turned, hidden[:, at], (1, 0))
        mine[:, at] = term.astype(BF16)
        grad_down[:, at] = jnp.zeros((rank, tile), F32)

    if staged:
        out = pltpu.make_async_copy(stage, parts.at[me], local_sems.at[3])
        out.start()
        out.wait()
    terms.begin()

    def chunk(offset, which):
        return chip_at(lax.rem(spot + offset + chips, chips)) * 2 + which

    def share(j):
        return (u_all[j][rank:rank + 1, 0:1].astype(F32) == me.astype(F32)).astype(F32)

    def add_terms(i, first):
        j = chunk(i // 2 + first, lax.rem(i, 2))
        weight_of = share(j)
        if staged:
            get = pltpu.make_async_copy(parts.at[j], stage, local_sems.at[3])
            get.start()
            get.wait()

        @pl.loop(0, width // tile)
        def _(t):
            at = pl.ds(pl.multiple_of(t * tile, tile), tile)
            term = stage[:, at] if staged else parts[j, :, at]
            grad_down[:, at] += weight_of * term.astype(F32)

    rows = w_all.shape[1]

    def apply_weight(i, total, first):
        j = chunk(i // 2 + first, lax.rem(i, 2))
        at = pl.ds(pl.multiple_of(j * rows, 128), rows)
        block = w_all[j]
        base = dot(gradient[...], block, (1, 1))
        grad_hidden[:, at] = (base + grad_hidden[:, at].astype(F32)).astype(BF16)
        return total + dot(hidden[:, at], block, (1, 0))

    for k in range(1, last + 1):
        downs.step(k)
        if k > 1:
            weights.step(k - 1)
            terms.step(k - 1)
        downs.cross(k)
        if k > 1:
            weights.cross(k - 1)
    for k in range(last + 1):
        downs.settle(k)

    def low_part(t, total):
        at = pl.ds(pl.multiple_of(t * tile, tile), tile)
        piece = d_all[slot, :, at]
        grad_hidden[:, at] = dot(back[...], piece, (1, 0)).astype(BF16)
        return total + dot(hidden[:, at], piece, (1, 1))

    low = lax.fori_loop(0, width // tile, low_part, jnp.zeros((hidden.shape[0], rank), F32))
    low_turned = low.astype(BF16).astype(F32).T.astype(BF16)
    t_all[me] = (adapter_scale * dot(low_turned, gradient[...], (1, 0))).astype(BF16)
    up_terms.begin()
    total = adapter_scale * dot(low.astype(BF16), u_all[slot][:rank, :], (1, 0))

    for k in range(1, last + 1):
        up_terms.step(k)
        if k == 1:
            weights.step(last)
            terms.step(last)
            weights.cross(last)
    for k in range(last):
        weights.settle(k)
        terms.settle(k)
    before = 2 * (2 * last - 1)
    total = lax.fori_loop(0, before, functools.partial(apply_weight, first=1 - last), total)

    @pl.loop(0, before)
    def _(i):
        add_terms(i, 1 - last)

    weights.settle(last)
    total = lax.fori_loop(0, 2, functools.partial(apply_weight, first=last), total)
    values[...] = total.astype(BF16)
    terms.settle(last)

    @pl.loop(0, 2)
    def _(i):
        add_terms(i, last)

    for k in range(last + 1):
        up_terms.settle(k)
    grad_up[...] = lax.fori_loop(
        0, n, lambda j, held: held + share(j) * t_all[j].astype(F32),
        jnp.zeros(grad_up.shape, F32),
    )
    for copy in sent:
        copy.wait_send()


def ring_order(chips):
    if chips == 8:
        return (
            lambda p: jnp.where(p < 4, 2 * p, 2 * (7 - p) + 1),
            lambda c: jnp.where(lax.rem(c, 2) == 0, c // 2, 7 - c // 2),
        )
    return (lambda p: p, lambda c: c)


def per_device(
    hidden,
    output_gradient,
    frozen_value_weight,
    adapter_down_maps,
    adapter_up_maps,
    owner,
    token_block_tenant,
):
    n = lax.axis_size("fsdp")
    chips = n // 2
    rows, width = hidden.shape
    outputs = output_gradient.shape[1]
    rank = adapter_down_maps.shape[2]
    tenants = owner.shape[0]
    staged = n > 16
    slot = jnp.sum(
        jnp.where(token_block_tenant[0, 0] == jnp.arange(tenants, dtype=jnp.int32), owner, 0)
    )
    up = jnp.concatenate(
        [adapter_up_maps[0], jnp.broadcast_to(slot.astype(BF16), (16, outputs))], axis=0
    )
    down = adapter_down_maps[0].T
    count = 2 * copies_of(chips, True) + 3 * copies_of(chips, False)
    vmem = pl.BlockSpec(memory_space=pltpu.VMEM)
    hbm = pl.BlockSpec(memory_space=pl.ANY)
    out_shape = [
        jax.ShapeDtypeStruct((rows, outputs), BF16),
        jax.ShapeDtypeStruct((rows, width), BF16),
        jax.ShapeDtypeStruct((rank, width), F32),
        jax.ShapeDtypeStruct((rank, outputs), F32),
    ]
    out_specs = [vmem] * 4
    scratch = []
    if staged:
        out_shape.append(jax.ShapeDtypeStruct((n, rank, width), BF16))
        out_specs.append(hbm)
    else:
        scratch.append(pltpu.VMEM((n, rank, width), BF16))
    scratch += [
        pltpu.VMEM((n,) + frozen_value_weight.shape, BF16),
        pltpu.VMEM((n, rank, width), BF16),
        pltpu.VMEM((n,) + up.shape, BF16),
        pltpu.VMEM((n, rank, outputs), BF16),
        pltpu.VMEM((rows, rank), BF16),
    ]
    if staged:
        scratch.append(pltpu.VMEM((rank, width), BF16))
    scratch += [
        pltpu.SemaphoreType.DMA((count,)),
        pltpu.SemaphoreType.DMA((count,)),
        pltpu.SemaphoreType.DMA((4,)),
    ]
    results = pl.pallas_call(
        functools.partial(kernel, n, ring_order(chips), staged),
        out_shape=out_shape,
        in_specs=[pl.BlockSpec(memory_space=pltpu.SMEM), vmem, vmem, hbm, hbm, hbm],
        out_specs=out_specs,
        scratch_shapes=scratch,
        compiler_params=pltpu.CompilerParams(
            collective_id=0, has_side_effects=True, vmem_limit_bytes=56 << 20
        ),
    )(slot.reshape(1), hidden, output_gradient, frozen_value_weight, down, up)
    values, grad_hidden, grad_down, grad_up = results[:4]
    return values, grad_hidden, grad_down.T[None], grad_up[None]


def solution(mesh):
    return jax.shard_map(
        per_device,
        mesh=mesh,
        in_specs=(
            P(("groups", "fsdp"), None),
            P(("groups", "fsdp"), None),
            P("fsdp", None),
            P("fsdp", None, None),
            P("fsdp", None, None),
            P(),
            P(("groups", "fsdp"), None),
        ),
        out_specs=(
            P(("groups", "fsdp"), None),
            P(("groups", "fsdp"), None),
            P(("groups", "fsdp"), None, None),
            P(("groups", "fsdp"), None, None),
        ),
        check_vma=False,
    )
```

time: 403 us -> 159 us (0.39)
  waiting for transfers between devices: 149 us -> 0 us
  Pallas kernels: 0 us -> 148 us
  blocking collectives: 85.9 us -> 0 us
  other arithmetic: 51.3 us -> 1.29 us
  local copies, waits for them, and re-layouts: 47.2 us -> 7.75 us
  starting transfers between devices: 34.3 us -> 0 us
  matrix products: 16.8 us -> 0 us
  between operations: 16.5 us -> 1.95 us
    pallas_call x0 -> x1, Pallas kernels: none -> 148 us  [per_device(): pl.pallas_call(functools.partial(kernel, n, ring_order(chips), staged), o...]
    all_to_all x4 -> x0, waiting for transfers between devices: 93 us -> none  [the longest x1 53.9 us: per_device(): lax.all_to_all(side_cols, 'fsdp', split_axis=0, concat_axis=1, tiled=True)]
    reduce_scatter x2 -> x0, waiting for transfers between devices: 50 us -> none  [the longest x1 50 us: per_device(): lax.psum_scatter(slot_up_map, 'fsdp', scatter_dimension=0, tiled=True)]
    unnamed x2 -> x0, other arithmetic: 48.7 us -> none
    unnamed x1 -> x0, blocking collectives: 47.3 us -> none
    all_gather x2 -> x0, blocking collectives: 38.6 us -> none  [the longest x1 20.8 us: per_device(): every_up_map = lax.all_gather(adapter_up_maps, 'fsdp', axis=0, tiled=True)]
    all_to_all x4 -> x0, starting transfers between devices: 34.2 us -> none  [the longest x1 18.1 us: per_device(): lax.all_to_all(slot_down, 'fsdp', split_axis=0, concat_axis=1, tiled=True)]
    unnamed x29 -> x8, local copies, waits for them, and re-layouts: 25.6 us -> 6.36 us
  transfers between devices with their start and end apart: 7 -> 0, of which waited for: 5 -> 0; matrix products, arithmetic and copies ran while one was open for 13% -> 0% of each run, Pallas kernels for 0% -> 0%
where the time goes in v1:
time: 159 us
  Pallas kernels  148 us (93%)
  local copies, waits for them, and re-layouts  7.75 us (5%)
  between operations  1.95 us (1%)
    pallas_call x1, Pallas kernels, per_device(): pl.pallas_call(functools.partial(kernel, n, ring_order(chips), staged), o...  148 us
    unnamed x8, local copies, waits for them, and re-layouts  6.36 us

profile of v1, /device:TPU:0, one launch (start us, length us, event | category | flops | bytes accessed | tf_op | source)
XLA Modules:
  0.0 158.8 jit_solution(9072163176576349168)
XLA Ops:
  1.3 1.3 fusion
  3.2 1.4 concatenate.3.up
  4.6 147.8 %shard_map.102 = (bf16[128,512]{1,0:T(8,128)(2,1)}, bf16[128,8192]{1,0:T(8,128)(2,1)}, f32[32,8192]{1,0:T(8,128)}, f32[32,512]{1,0:T(8,128)}) custom-call(s32[1]{0:T(128)} %bitcast.1.slot_ref, bf16[128,8192]{1,0:T(8,128)(2,1)} %hidden.1, bf16[128,512]{1,0:T(8,128)(2,1)} %gradient.1, bf16[512,512]{1,0:T(8,128)(2,1)} %weight.1, bf16[32,8192]{1,0:T(8,128)(2,1)} %bitcast.12, ...), custom_call_target="tpu_custom_call" | custom-call | tf_op jit(solution)/shard_map/pallas_call | solution.py:332
  152.4 1.6 copy.16
  154.0 0.0 copy-start
  154.0 0.0 copy-start.1
  154.0 3.2 %copy.17 = bf16[128,8192]{1,0:T(8,128)(2,1)} copy(bf16[128,8192]{1,0:T(8,128)(2,1)} %get-tuple-element.17) | data formatting | bytes 4194304
  157.2 0.0 copy-done
  157.2 1.0 copy.18
  158.2 0.0 copy-done.1
  158.2 0.6 copy.19
Async XLA Ops:
  154.0 3.2 %copy-start = (f32[32,8192]{1,0:T(8,128)S(1)}, f32[32,8192]{1,0:T(8,128)}, u32[]{:S(2)}) copy-start(f32[32,8192]{1,0:T(8,128)} %get-tuple-element.10) | copy-start | bytes 3145732
  154.0 4.2 %copy-start.1 = (f32[32,512]{1,0:T(8,128)S(1)}, f32[32,512]{1,0:T(8,128)}, u32[]{:S(2)}) copy-start(f32[32,512]{1,0:T(8,128)} %get-tuple-element.11) | copy-start | bytes 196612

commit v2 on v1

--- a/solution.py
+++ b/solution.py
@@ -50,7 +50,7 @@
         self.right[1] = self.send(place["me"], self.start_at, self.length, place["right"])
         self.left[1] = self.send(place["me"], self.start_at, self.length, place["left"])
 
-    def step(self, k):
+    def step(self, k, hold_twin=False):
         place, half = self.place, self.length // 2
         last = place["chips"] // 2
         from_left, from_right = self.mine(-k), self.mine(k)
@@ -65,13 +65,19 @@
                 from_right, self.start_at + self.length - size, size, place["left"]
             )
         got = [from_left, from_right] if k < last else [from_left]
-        if self.shared:
-            self.twin[k] = [self.send(i, self.start_at, self.length, place["twin"]) for i in got]
+        if self.shared and not hold_twin:
+            self.to_twin(k)
         self.near[k] = [self.send(i, self.start_at, self.length, place["near"]) for i in got]
 
+    def got(self, k):
+        return [self.mine(-k), self.mine(k)] if k < self.place["chips"] // 2 else [self.mine(-k)]
+
+    def to_twin(self, k):
+        to = self.place["twin"]
+        self.twin[k] = [self.send(i, self.start_at, self.length, to) for i in self.got(k)]
+
     def cross(self, k):
-        place, last = self.place, self.place["chips"] // 2
-        got = [self.mine(-k), self.mine(k)] if k < last else [self.mine(-k)]
+        place, got = self.place, self.got(k)
         self.near_twin[k] = []
         for i, copy in zip(got, self.twin[k]):
             copy.wait_recv()
@@ -81,6 +87,29 @@
         for copy in self.near[k]:
             copy.wait_recv()
         for copy in self.near_twin.get(k, []):
+            copy.wait_recv()
+
+
+class Direct:
+    def __init__(self, place, pool, buf):
+        self.place, self.pool, self.buf = place, pool, buf
+
+    def begin(self):
+        place = self.place
+        ref = self.buf.at[place["me"]]
+        self.far = [self.pool(ref, to) for to in place["peers"]]
+        self.near = [self.pool(ref, place["near"])]
+
+    def pass_on(self):
+        chips = self.place["chips"]
+        for offset, copy in enumerate(self.far, 1):
+            copy.wait_recv()
+            spot = lax.rem(self.place["spot"] - offset + chips, chips)
+            ref = self.buf.at[self.place["chip_at"](spot) * 2 + self.place["core"]]
+            self.near.append(self.pool(ref, self.place["near"]))
+
+    def settle(self):
+        for copy in self.near:
             copy.wait_recv()
 
 
@@ -110,8 +139,9 @@
     def device(at):
         return (group, chip_at(lax.rem(spot + at + chips, chips)) * 2 + core)
 
+    peers = [device(at) for at in range(1, chips)]
     place = {
-        "me": me, "core": core, "spot": spot, "side": side, "chips": chips, "chip_at": chip_at,
+        "peers": peers, "me": me, "core": core, "spot": spot, "side": side, "chips": chips, "chip_at": chip_at,
         "right": device(1), "left": device(-1),
         "near": (group, chip * 2 + 1 - core), "twin": (group + 1 - 2 * side, me),
     }
@@ -123,9 +153,10 @@
         copy.start()
 
     barrier = pltpu.get_barrier_semaphore()
-    for to in ("right", "left", "near", "twin"):
-        pl.semaphore_signal(barrier, inc=1, device_id=place[to], device_id_type=MESH)
-    pl.semaphore_wait(barrier, 4)
+    greeted = [*peers, place["near"], place["twin"]]
+    for to in greeted:
+        pl.semaphore_signal(barrier, inc=1, device_id=to, device_id_type=MESH)
+    pl.semaphore_wait(barrier, len(greeted))
 
     sent = []
 
@@ -139,28 +170,26 @@
         sent.append(copy)
         return copy
 
-    ups = Ring(place, pool, u_all, 2, False)
+    ups = Direct(place, pool, u_all)
     downs = Ring(place, pool, d_all, 2, True)
     weights = Ring(place, pool, w_all, 1, True)
     terms = Ring(place, pool, parts, 2, False)
-    up_terms = Ring(place, pool, t_all, 2, False)
+    up_terms = Direct(place, pool, t_all)
 
     local[0].wait()
     ups.begin()
     local[1].wait()
     downs.begin()
-    for k in range(1, last + 1):
-        ups.step(k)
-        if k == 1:
-            local[2].wait()
-            weights.begin()
-    for k in range(last + 1):
-        ups.settle(k)
+    local[2].wait()
+    weights.begin()
+    ups.pass_on()
+    ups.settle()
 
     rank, width = down.shape
+    outputs = gradient.shape[1]
     tile = 1024
     slot = slot_ref[0]
-    up_slot = u_all[slot][:rank, :]
+    up_slot = u_all[slot][:, :outputs]
     back_low = (adapter_scale * dot(gradient[...], up_slot, (1, 1))).astype(BF16)
     back[...] = back_low
     back_turned = back_low.astype(F32).T.astype(BF16)
@@ -177,13 +206,14 @@
         out = pltpu.make_async_copy(stage, parts.at[me], local_sems.at[3])
         out.start()
         out.wait()
+    downs.step(1)
     terms.begin()
 
     def chunk(offset, which):
         return chip_at(lax.rem(spot + offset + chips, chips)) * 2 + which
 
     def share(j):
-        return (u_all[j][rank:rank + 1, 0:1].astype(F32) == me.astype(F32)).astype(F32)
+        return (u_all[j][0:1, outputs:outputs + 1].astype(F32) == me.astype(F32)).astype(F32)
 
     def add_terms(i, first):
         j = chunk(i // 2 + first, lax.rem(i, 2))
@@ -209,14 +239,20 @@
         grad_hidden[:, at] = (base + grad_hidden[:, at].astype(F32)).astype(BF16)
         return total + dot(hidden[:, at], block, (1, 0))
 
-    for k in range(1, last + 1):
+    downs.step(2)
+    weights.step(1)
+    downs.cross(1)
+    for k in range(3, last + 1):
         downs.step(k)
-        if k > 1:
-            weights.step(k - 1)
-            terms.step(k - 1)
-        downs.cross(k)
-        if k > 1:
-            weights.cross(k - 1)
+        if k > 3:
+            weights.to_twin(k - 2)
+        terms.step(k - 2)
+        weights.step(k - 1, hold_twin=True)
+        downs.cross(k - 1)
+        if k > 3:
+            weights.cross(k - 3)
+    weights.to_twin(last - 1)
+    downs.cross(last)
     for k in range(last + 1):
         downs.settle(k)
 
@@ -230,35 +266,40 @@
     low_turned = low.astype(BF16).astype(F32).T.astype(BF16)
     t_all[me] = (adapter_scale * dot(low_turned, gradient[...], (1, 0))).astype(BF16)
     up_terms.begin()
-    total = adapter_scale * dot(low.astype(BF16), u_all[slot][:rank, :], (1, 0))
-
-    for k in range(1, last + 1):
-        up_terms.step(k)
-        if k == 1:
-            weights.step(last)
-            terms.step(last)
-            weights.cross(last)
-    for k in range(last):
+    total = adapter_scale * dot(low.astype(BF16), u_all[slot][:, :outputs], (1, 0))
+
+    def use(total, first, offsets):
+        total = lax.fori_loop(
+            0, 2 * offsets, functools.partial(apply_weight, first=first), total
+        )
+
+        @pl.loop(0, 2 * offsets)
+        def _(i):
+            add_terms(i, first)
+
+        return total
+
+    for k in range(last - 2):
         weights.settle(k)
         terms.settle(k)
-    before = 2 * (2 * last - 1)
-    total = lax.fori_loop(0, before, functools.partial(apply_weight, first=1 - last), total)
-
-    @pl.loop(0, before)
-    def _(i):
-        add_terms(i, 1 - last)
-
-    weights.settle(last)
-    total = lax.fori_loop(0, 2, functools.partial(apply_weight, first=last), total)
+    total = use(total, 3 - last, 2 * last - 5)
+    terms.step(last - 1)
+    weights.cross(last - 2)
+    weights.step(last)
+    weights.settle(last - 2)
+    terms.settle(last - 2)
+    total = use(total, last - 2, 1)
+    total = use(total, 2 - last, 1)
+    terms.step(last)
+    up_terms.pass_on()
+    weights.cross(last - 1)
+    weights.cross(last)
+    for k in (last - 1, last):
+        weights.settle(k)
+        terms.settle(k)
+    total = use(total, last - 1, 3)
     values[...] = total.astype(BF16)
-    terms.settle(last)
-
-    @pl.loop(0, 2)
-    def _(i):
-        add_terms(i, last)
-
-    for k in range(last + 1):
-        up_terms.settle(k)
+    up_terms.settle()
     grad_up[...] = lax.fori_loop(
         0, n, lambda j, held: held + share(j) * t_all[j].astype(F32),
         jnp.zeros(grad_up.shape, F32),
@@ -296,10 +337,10 @@
         jnp.where(token_block_tenant[0, 0] == jnp.arange(tenants, dtype=jnp.int32), owner, 0)
     )
     up = jnp.concatenate(
-        [adapter_up_maps[0], jnp.broadcast_to(slot.astype(BF16), (16, outputs))], axis=0
+        [adapter_up_maps[0], jnp.broadcast_to(slot.astype(BF16), (rank, 128))], axis=1
     )
     down = adapter_down_maps[0].T
-    count = 2 * copies_of(chips, True) + 3 * copies_of(chips, False)
+    count = 2 * copies_of(chips, True) + copies_of(chips, False) + 2 * (2 * chips - 1)
     vmem = pl.BlockSpec(memory_space=pltpu.VMEM)
     hbm = pl.BlockSpec(memory_space=pl.ANY)
     out_shape = [

time: 159 us -> 123 us (0.77); the launches traced: 159 us -> 121 us
  Pallas kernels: 148 us -> 110 us
    pallas_call x1, Pallas kernels: 148 us -> 110 us  [per_device(): pl.pallas_call(functools.partial(kernel, n, ring_order(chips), staged), o...]
where the time goes in v2:
time: 123 us; the launch traced here: 121 us
  Pallas kernels  110 us (89%)
  local copies, waits for them, and re-layouts  7.74 us (6%)
  between operations  1.95 us (2%)
  other arithmetic  1.29 us (1%)
    pallas_call x1, Pallas kernels, per_device(): pl.pallas_call(functools.partial(kernel, n, ring_order(chips), staged), o...  110 us
    unnamed x8, local copies, waits for them, and re-layouts  6.36 us

profile of v2, /device:TPU:0, one launch (start us, length us, event | category | flops | bytes accessed | tf_op | source)
XLA Modules:
  0.0 121.1 jit_solution(118780134721016930)
XLA Ops:
  1.3 1.3 %fusion = s32[]{:T(128)} fusion(s32[16]{0:T(128)} %param.12, s32[]{:T(128)} %bitcast.10), kind=kLoop, calls=%fused_computation.1 | loop fusion | flops 47 | bytes 72 | tf_op jit(solution)/shard_map/reduce_sum | solution.py:336
  3.2 1.4 %concatenate.3.up = bf16[32,640]{1,0:T(8,128)(2,1)} pad(bf16[32,512]{1,0:T(8,128)(2,1)} %bitcast.14, bf16[]{:T(256)S(6)} %convert_element_type.3), padding=0_0x0_128 | pad | bytes 73730 | tf_op jit(solution)/shard_map/concatenate | solution.py:339
  4.6 110.1 %shard_map.102 = (bf16[128,512]{1,0:T(8,128)(2,1)}, bf16[128,8192]{1,0:T(8,128)(2,1)}, f32[32,8192]{1,0:T(8,128)}, f32[32,512]{1,0:T(8,128)}) custom-call(s32[1]{0:T(128)} %bitcast.1.slot_ref, bf16[128,8192]{1,0:T(8,128)(2,1)} %hidden.1, bf16[128,512]{1,0:T(8,128)(2,1)} %gradient.1, bf16[512,512]{1,0:T(8,128)(2,1)} %weight.1, bf16[32,8192]{1,0:T(8,128)(2,1)} %bitcast.12, ...), custom_call_target="tpu_custom_call" | custom-call | tf_op jit(solution)/shard_map/pallas_call | solution.py:373
  114.7 1.6 %copy.16 = bf16[128,512]{1,0:T(8,128)(2,1)} copy(bf16[128,512]{1,0:T(8,128)(2,1)} %get-tuple-element.16) | data formatting | bytes 262144
  116.3 0.0 copy-start
  116.3 0.0 copy-start.1
  116.3 3.2 %copy.17 = bf16[128,8192]{1,0:T(8,128)(2,1)} copy(bf16[128,8192]{1,0:T(8,128)(2,1)} %get-tuple-element.17) | data formatting | bytes 4194304
  119.5 0.0 copy-done
  119.5 1.0 copy.18
  120.4 0.0 copy-done.1
  120.4 0.6 copy.19
Async XLA Ops:
  116.3 3.2 %copy-start = (f32[32,8192]{1,0:T(8,128)S(1)}, f32[32,8192]{1,0:T(8,128)}, u32[]{:S(2)}) copy-start(f32[32,8192]{1,0:T(8,128)} %get-tuple-element.10) | copy-start | bytes 3145732
  116.3 4.2 %copy-start.1 = (f32[32,512]{1,0:T(8,128)S(1)}, f32[32,512]{1,0:T(8,128)}, u32[]{:S(2)}) copy-start(f32[32,512]{1,0:T(8,128)} %get-tuple-element.11) | copy-start | bytes 196612

commit v3 on v2

--- a/solution.py
+++ b/solution.py
@@ -22,8 +22,11 @@
         self.place, self.pool, self.buf, self.axis = place, pool, buf, axis
         length = buf.shape[axis]
         self.shared = shared
-        self.length = length // 2 if shared else length
-        self.start_at = place["side"] * self.length if shared else 0
+        unit = 32 if axis == 1 else 256
+        self.length = max(length // 2, length * 9 // 16 // unit * unit) if shared else length
+        self.swapped = length - self.length
+        self.start_at = place["side"] * self.swapped if shared else 0
+        self.out_at = place["side"] * self.length if shared else 0
         self.other_at = (1 - place["side"]) * self.length if shared else 0
         self.right, self.left, self.twin, self.near = {}, {}, {}, {}
         self.near_twin = {}
@@ -74,20 +77,173 @@
 
     def to_twin(self, k):
         to = self.place["twin"]
-        self.twin[k] = [self.send(i, self.start_at, self.length, to) for i in self.got(k)]
+        self.twin[k] = [self.send(i, self.out_at, self.swapped, to) for i in self.got(k)]
 
     def cross(self, k):
         place, got = self.place, self.got(k)
         self.near_twin[k] = []
         for i, copy in zip(got, self.twin[k]):
             copy.wait_recv()
-            self.near_twin[k].append(self.send(i, self.other_at, self.length, place["near"]))
+            self.near_twin[k].append(self.send(i, self.other_at, self.swapped, place["near"]))
 
     def settle(self, k):
         for copy in self.near[k]:
             copy.wait_recv()
         for copy in self.near_twin.get(k, []):
             copy.wait_recv()
+
+
+class Lanes:
+    def __init__(self, place, make, parts, sums_in, sums_out, cross_in, cross_out):
+        core, chip = place["core"], place["chip"]
+        self.place, self.parts = place, parts
+        self.sums_in, self.sums_out = sums_in, sums_out
+        self.cross_in, self.cross_out = cross_in, cross_out
+        group, me = place["group"], place["me"]
+        z, y = chip // 2, lax.rem(chip, 2)
+        self.z, self.y = z, y
+        self.inner = (z == 1) | (z == 2)
+        self.outer = jnp.logical_not(self.inner)
+        self.z_out = jnp.where(z < 2, 0, 3)
+        z_in = jnp.where(self.inner, 3 - z, jnp.where(z == 0, 1, 2))
+
+        def at(where_z, where_y, which):
+            return (where_z * 2 + where_y) * 2 + which
+
+        self.at = at
+        inward, outward = (group, at(z_in, y, core)), (group, at(self.z_out, y, core))
+        near, across = place["near"], (group, at(z, 1 - y, core))
+
+        def block(j, to):
+            return make(parts.at[j], parts.at[j], to)
+
+        behind, facing = at(self.z_out, y, core), at(3 - z, y, core)
+        far = at(3 - self.z_out, y, core)
+        self.own_near = block(me, near)
+        self.first, self.second = block(me, inward), block(me, inward)
+        self.relay = block(behind, inward)
+        self.near = [block(j, near) for j in (behind, facing, far)]
+        self.sums = [make(sums_out.at[i], sums_in.at[i], outward) for i in range(2)]
+        self.cross = make(cross_out, cross_in, across)
+
+    def begin(self):
+        self.own_near.start()
+
+        @pl.when(self.outer)
+        def _():
+            self.first.start()
+
+        @pl.when(self.inner)
+        def _():
+            self.second.start()
+
+    def relay_on(self):
+        @pl.when(self.inner)
+        def _():
+            self.first.wait_recv()
+            self.relay.start()
+            self.near[0].start()
+
+    def facing_in(self):
+        @pl.when(self.inner)
+        def _():
+            self.second.wait_recv()
+            self.near[1].start()
+
+    def far_in(self):
+        @pl.when(self.inner)
+        def _():
+            self.relay.wait_recv()
+            self.near[2].start()
+
+    def over_tiles(self, body):
+        width, tile = self.parts.shape[2], 1024
+
+        @pl.loop(0, width // tile)
+        def _(t):
+            body(pl.ds(pl.multiple_of(t * tile, tile), tile))
+
+    def add(self, blocks, share, slots):
+        weights = [[share(j, slot) for j in blocks] for slot in slots]
+
+        def at_tile(at):
+            terms = [self.parts[j, :, at].astype(F32) for j in blocks]
+            return [sum(w * term for w, term in zip(row, terms)) for row in weights]
+
+        return at_tile
+
+    def sum_inner(self, share, mine_ref):
+        place, at = self.place, self.at
+        me, core = place["me"], place["core"]
+        z, y = self.z, self.y
+
+        @pl.when(self.inner)
+        def _():
+            self.own_near.wait_recv()
+            for copy in self.near:
+                copy.wait_recv()
+            rest = [at(q, y, c) for q in (z, 3 - z, 3 - self.z_out) for c in (0, 1)]
+            outward = self.add(rest, share, [at(self.z_out, i, core) for i in (0, 1)])
+
+            def body(tile):
+                for i, total in enumerate(outward(tile)):
+                    self.sums_out[i, :, tile] = total.astype(BF16)
+
+            self.over_tiles(body)
+            for copy in self.sums:
+                copy.start()
+            row = [at(q, y, c) for q in range(4) for c in (0, 1)]
+            column = self.add(row, share, [me, at(z, 1 - y, core)])
+
+            def body(tile):
+                held, other = column(tile)
+                mine_ref[:, tile] = held
+                self.cross_out[:, tile] = other.astype(BF16)
+
+            self.over_tiles(body)
+            self.cross.start()
+
+    def sum_outer(self, share, mine_ref):
+        place, at = self.place, self.at
+        me, core = place["me"], place["core"]
+        z, y = self.z, self.y
+
+        @pl.when(self.outer)
+        def _():
+            self.own_near.wait_recv()
+            for copy in self.sums:
+                copy.wait_recv()
+            column = self.add([at(z, y, c) for c in (0, 1)], share, [me, at(z, 1 - y, core)])
+
+            def body(tile):
+                held, other = column(tile)
+                mine_ref[:, tile] = held + self.sums_in[y, :, tile].astype(F32)
+                other = other + self.sums_in[1 - y, :, tile].astype(F32)
+                self.cross_out[:, tile] = other.astype(BF16)
+
+            self.over_tiles(body)
+            self.cross.start()
+
+    def finish(self, mine_ref):
+        self.cross.wait_recv()
+
+        def body(tile):
+            mine_ref[:, tile] += self.cross_in[:, tile].astype(F32)
+
+        self.over_tiles(body)
+
+    def drain(self):
+        self.own_near.wait_send()
+        self.cross.wait_send()
+
+        @pl.when(self.outer)
+        def _():
+            self.first.wait_send()
+
+        @pl.when(self.inner)
+        def _():
+            for copy in (self.second, self.relay, *self.near, *self.sums):
+                copy.wait_send()
 
 
 class Direct:
@@ -121,13 +277,13 @@
 
 def kernel(
     n, ring_of, staged,
-    slot_ref, hidden, gradient, weight, down, up,
+    owner, tenant, hidden, gradient, weight, down, up,
     values, grad_hidden, grad_down, grad_up, *rest,
 ):
-    if staged:
-        parts, w_all, d_all, u_all, t_all, back, stage, send_sems, recv_sems, local_sems = rest
-    else:
-        parts, w_all, d_all, u_all, t_all, back, send_sems, recv_sems, local_sems = rest
+    lanes_used = n == 16
+    parts, w_all, d_all, u_all, t_all, back = rest[:6]
+    send_sems, recv_sems, local_sems = rest[-3:]
+    stage = rest[6] if staged else None
     me = lax.axis_index("fsdp")
     group = lax.axis_index("groups")
     chips, last = n // 2, n // 4
@@ -141,16 +297,24 @@
 
     peers = [device(at) for at in range(1, chips)]
     place = {
-        "peers": peers, "me": me, "core": core, "spot": spot, "side": side, "chips": chips, "chip_at": chip_at,
+        "peers": peers, "me": me, "group": group, "chip": chip, "core": core, "spot": spot, "side": side, "chips": chips, "chip_at": chip_at,
         "right": device(1), "left": device(-1),
         "near": (group, chip * 2 + 1 - core), "twin": (group + 1 - 2 * side, me),
     }
     local = [
         pltpu.make_async_copy(src, dst.at[me], local_sems.at[i])
-        for i, (src, dst) in enumerate(((up, u_all), (down, d_all), (weight, w_all)))
+        for i, (src, dst) in enumerate(((down, d_all), (weight, w_all)))
     ]
     for copy in local:
         copy.start()
+
+    slot = jnp.int32(0)
+    for t in range(owner.shape[0]):
+        slot = slot + jnp.where(tenant[0, 0] == t, owner[t], 0)
+    rank, width = down.shape
+    outputs = gradient.shape[1]
+    u_all[me, :, :outputs] = up[...]
+    u_all[me, :, outputs:] = jnp.broadcast_to(slot.astype(F32), (rank, 128)).astype(BF16)
 
     barrier = pltpu.get_barrier_semaphore()
     greeted = [*peers, place["near"], place["twin"]]
@@ -160,12 +324,18 @@
 
     sent = []
 
-    def pool(ref, to):
-        i = len(sent)
-        copy = pltpu.make_async_remote_copy(
-            src_ref=ref, dst_ref=ref, send_sem=send_sems.at[i], recv_sem=recv_sems.at[i],
+    made = []
+
+    def make(src, dst, to):
+        i = len(made)
+        made.append(i)
+        return pltpu.make_async_remote_copy(
+            src_ref=src, dst_ref=dst, send_sem=send_sems.at[i], recv_sem=recv_sems.at[i],
             device_id=to, device_id_type=MESH,
         )
+
+    def pool(ref, to):
+        copy = make(ref, ref, to)
         copy.start()
         sent.append(copy)
         return copy
@@ -173,22 +343,21 @@
     ups = Direct(place, pool, u_all)
     downs = Ring(place, pool, d_all, 2, True)
     weights = Ring(place, pool, w_all, 1, True)
-    terms = Ring(place, pool, parts, 2, False)
+    if lanes_used:
+        terms = Lanes(place, make, parts, *rest[6:10])
+    else:
+        terms = Ring(place, pool, parts, 2, False)
     up_terms = Direct(place, pool, t_all)
 
+    ups.begin()
     local[0].wait()
-    ups.begin()
+    downs.begin()
     local[1].wait()
-    downs.begin()
-    local[2].wait()
     weights.begin()
     ups.pass_on()
     ups.settle()
 
-    rank, width = down.shape
-    outputs = gradient.shape[1]
     tile = 1024
-    slot = slot_ref[0]
     up_slot = u_all[slot][:, :outputs]
     back_low = (adapter_scale * dot(gradient[...], up_slot, (1, 1))).astype(BF16)
     back[...] = back_low
@@ -212,8 +381,8 @@
     def chunk(offset, which):
         return chip_at(lax.rem(spot + offset + chips, chips)) * 2 + which
 
-    def share(j):
-        return (u_all[j][0:1, outputs:outputs + 1].astype(F32) == me.astype(F32)).astype(F32)
+    def share(j, to=me):
+        return (u_all[j][0:1, outputs:outputs + 1].astype(F32) == to.astype(F32)).astype(F32)
 
     def add_terms(i, first):
         j = chunk(i // 2 + first, lax.rem(i, 2))
@@ -246,7 +415,12 @@
         downs.step(k)
         if k > 3:
             weights.to_twin(k - 2)
-        terms.step(k - 2)
+        if not lanes_used:
+            terms.step(k - 2)
+        elif k == 3:
+            terms.relay_on()
+        else:
+            terms.facing_in()
         weights.step(k - 1, hold_twin=True)
         downs.cross(k - 1)
         if k > 3:
@@ -273,30 +447,42 @@
             0, 2 * offsets, functools.partial(apply_weight, first=first), total
         )
 
-        @pl.loop(0, 2 * offsets)
-        def _(i):
-            add_terms(i, first)
+        if not lanes_used:
+
+            @pl.loop(0, 2 * offsets)
+            def _(i):
+                add_terms(i, first)
 
         return total
 
     for k in range(last - 2):
         weights.settle(k)
-        terms.settle(k)
+        if not lanes_used:
+            terms.settle(k)
+    if lanes_used:
+        terms.far_in()
+        terms.sum_inner(share, grad_down)
     total = use(total, 3 - last, 2 * last - 5)
-    terms.step(last - 1)
+    if not lanes_used:
+        terms.step(last - 1)
     weights.cross(last - 2)
     weights.step(last)
     weights.settle(last - 2)
-    terms.settle(last - 2)
+    if not lanes_used:
+        terms.settle(last - 2)
     total = use(total, last - 2, 1)
     total = use(total, 2 - last, 1)
-    terms.step(last)
+    if lanes_used:
+        terms.sum_outer(share, grad_down)
+    else:
+        terms.step(last)
     up_terms.pass_on()
     weights.cross(last - 1)
     weights.cross(last)
     for k in (last - 1, last):
         weights.settle(k)
-        terms.settle(k)
+        if not lanes_used:
+            terms.settle(k)
     total = use(total, last - 1, 3)
     values[...] = total.astype(BF16)
     up_terms.settle()
@@ -304,6 +490,9 @@
         0, n, lambda j, held: held + share(j) * t_all[j].astype(F32),
         jnp.zeros(grad_up.shape, F32),
     )
+    if lanes_used:
+        terms.finish(grad_down)
+        terms.drain()
     for copy in sent:
         copy.wait_send()
 
@@ -331,17 +520,11 @@
     rows, width = hidden.shape
     outputs = output_gradient.shape[1]
     rank = adapter_down_maps.shape[2]
-    tenants = owner.shape[0]
     staged = n > 16
-    slot = jnp.sum(
-        jnp.where(token_block_tenant[0, 0] == jnp.arange(tenants, dtype=jnp.int32), owner, 0)
-    )
-    up = jnp.concatenate(
-        [adapter_up_maps[0], jnp.broadcast_to(slot.astype(BF16), (rank, 128))], axis=1
-    )
     down = adapter_down_maps[0].T
     count = 2 * copies_of(chips, True) + copies_of(chips, False) + 2 * (2 * chips - 1)
     vmem = pl.BlockSpec(memory_space=pltpu.VMEM)
+    smem = pl.BlockSpec(memory_space=pltpu.SMEM)
     hbm = pl.BlockSpec(memory_space=pl.ANY)
     out_shape = [
         jax.ShapeDtypeStruct((rows, outputs), BF16),
@@ -359,12 +542,15 @@
     scratch += [
         pltpu.VMEM((n,) + frozen_value_weight.shape, BF16),
         pltpu.VMEM((n, rank, width), BF16),
-        pltpu.VMEM((n,) + up.shape, BF16),
+        pltpu.VMEM((n, rank, outputs + 128), BF16),
         pltpu.VMEM((n, rank, outputs), BF16),
         pltpu.VMEM((rows, rank), BF16),
     ]
     if staged:
         scratch.append(pltpu.VMEM((rank, width), BF16))
+    elif n == 16:
+        pair, single = pltpu.VMEM((2, rank, width), BF16), pltpu.VMEM((rank, width), BF16)
+        scratch += [pair, pair, single, single]
     scratch += [
         pltpu.SemaphoreType.DMA((count,)),
         pltpu.SemaphoreType.DMA((count,)),
@@ -373,13 +559,16 @@
     results = pl.pallas_call(
         functools.partial(kernel, n, ring_order(chips), staged),
         out_shape=out_shape,
-        in_specs=[pl.BlockSpec(memory_space=pltpu.SMEM), vmem, vmem, hbm, hbm, hbm],
+        in_specs=[smem, smem, vmem, vmem, hbm, hbm, vmem],
         out_specs=out_specs,
         scratch_shapes=scratch,
         compiler_params=pltpu.CompilerParams(
             collective_id=0, has_side_effects=True, vmem_limit_bytes=56 << 20
         ),
-    )(slot.reshape(1), hidden, output_gradient, frozen_value_weight, down, up)
+    )(
+        owner, token_block_tenant, hidden, output_gradient, frozen_value_weight, down,
+        adapter_up_maps[0],
+    )
     values, grad_hidden, grad_down, grad_up = results[:4]
     return values, grad_hidden, grad_down.T[None], grad_up[None]
 

time: 123 us -> 139 us (1.13); the launches traced: 121 us -> 139 us
  Pallas kernels: 110 us -> 131 us
    pallas_call x1, Pallas kernels: 110 us -> 131 us  [per_device(): pl.pallas_call(functools.partial(kernel, n, ring_order(chips), staged), o...]
where the time goes in v3:
time: 139 us
  Pallas kernels  131 us (94%)
  local copies, waits for them, and re-layouts  6.36 us (5%)
    pallas_call x1, Pallas kernels, per_device(): pl.pallas_call(functools.partial(kernel, n, ring_order(chips), staged), o...  131 us
    unnamed x8, local copies, waits for them, and re-layouts  6.36 us

profile of v3, /device:TPU:0, one launch (start us, length us, event | category | flops | bytes accessed | tf_op | source)
XLA Modules:
  0.0 138.6 jit_solution(16289951902769138492)
XLA Ops:
  1.3 130.9 %shard_map.102 = (bf16[128,512]{1,0:T(8,128)(2,1)}, bf16[128,8192]{1,0:T(8,128)(2,1)}, f32[32,8192]{1,0:T(8,128)}, f32[32,512]{1,0:T(8,128)}) custom-call(s32[16]{0:T(128)} %owner.1, s32[1,1]{1,0:T(1,128)S(6)} %copy.15.tenant, bf16[128,8192]{1,0:T(8,128)(2,1)} %hidden.1, bf16[128,512]{1,0:T(8,128)(2,1)} %gradient.1, bf16[512,512]{1,0:T(8,128)(2,1)} %weight.1, ...), custom_call_target="tpu_custom_call" | custom-call | tf_op jit(solution)/shard_map/pallas_call | solution.py:559
  132.2 1.6 %copy.16 = bf16[128,512]{1,0:T(8,128)(2,1)} copy(bf16[128,512]{1,0:T(8,128)(2,1)} %get-tuple-element.16) | data formatting | bytes 262144
  133.8 0.0 copy-start
  133.8 0.0 copy-start.1
  133.8 3.2 %copy.17 = bf16[128,8192]{1,0:T(8,128)(2,1)} copy(bf16[128,8192]{1,0:T(8,128)(2,1)} %get-tuple-element.17) | data formatting | bytes 4194304
  137.0 0.0 copy-done
  137.0 1.0 copy.18
  138.0 0.0 copy-done.1
  138.0 0.6 copy.19
Async XLA Ops:
  133.8 3.2 %copy-start = (f32[32,8192]{1,0:T(8,128)S(1)}, f32[32,8192]{1,0:T(8,128)}, u32[]{:S(2)}) copy-start(f32[32,8192]{1,0:T(8,128)} %get-tuple-element.10) | copy-start | bytes 3145732
  133.8 4.2 %copy-start.1 = (f32[32,512]{1,0:T(8,128)S(1)}, f32[32,512]{1,0:T(8,128)}, u32[]{:S(2)}) copy-start(f32[32,512]{1,0:T(8,128)} %get-tuple-element.11) | copy-start | bytes 196612

commit v4 on v2

--- a/solution.py
+++ b/solution.py
@@ -33,9 +33,9 @@
             return self.buf.at[index, pl.ds(pl.multiple_of(start, 16), length), :]
         return self.buf.at[index, :, pl.ds(pl.multiple_of(start, 128), length)]
 
-    def send(self, index, start, length, to):
+    def send(self, index, start, length, to, only=None):
         ref = self.view(index, start, length)
-        return self.pool(ref, to)
+        return self.pool(ref, to, only)
 
     def chip(self, offset):
         place = self.place
@@ -52,19 +52,34 @@
 
     def step(self, k, hold_twin=False):
         place, half = self.place, self.length // 2
-        last = place["chips"] // 2
+        last, short = place["chips"] // 2, place["short"]
         from_left, from_right = self.mine(-k), self.mine(k)
-        self.right[k].wait_recv()
-        if k + 1 <= last:
-            size = self.length if k + 1 < last else half
-            self.right[k + 1] = self.send(from_left, self.start_at, size, place["right"])
-        self.left[k].wait_recv()
-        if k + 1 <= last:
-            size = self.length if k + 1 < last else half
-            self.left[k + 1] = self.send(
-                from_right, self.start_at + self.length - size, size, place["left"]
+
+        def onward(spot, index, offset, to):
+            if k + 1 < last:
+                return self.send(index, self.start_at, self.length, to)
+            only = jnp.logical_not(place["inner"](spot)) if short else None
+            return self.send(index, self.start_at + offset, half, to, only)
+
+        def arrive(copy):
+            if k == last and short:
+                pl.when(jnp.logical_not(place["inner"](0)))(copy.wait_recv)
+            else:
+                copy.wait_recv()
+
+        arrive(self.right[k])
+        if k < last:
+            self.right[k + 1] = onward(1, from_left, 0, place["right"])
+        arrive(self.left[k])
+        if k < last:
+            self.left[k + 1] = onward(-1, from_right, self.length - half, place["left"])
+        if short and k == 1:
+            self.across = self.send(
+                place["facing"], self.start_at, self.length, place["across"], place["inner"](0)
             )
-        got = [from_left, from_right] if k < last else [from_left]
+        if short and k == last:
+            pl.when(place["inner"](0))(self.across.wait_recv)
+        got = self.got(k)
         if self.shared and not hold_twin:
             self.to_twin(k)
         self.near[k] = [self.send(i, self.start_at, self.length, place["near"]) for i in got]
@@ -116,12 +131,12 @@
 def copies_of(chips, shared):
     last = chips // 2
     got = 2 * last - 1
-    return 1 + 2 * last + got * (3 if shared else 1)
+    return 2 + 2 * last + got * (3 if shared else 1)
 
 
 def kernel(
     n, ring_of, staged,
-    slot_ref, hidden, gradient, weight, down, up,
+    owner, tenant, hidden, gradient, weight, down, up,
     values, grad_hidden, grad_down, grad_up, *rest,
 ):
     if staged:
@@ -140,17 +155,34 @@
         return (group, chip_at(lax.rem(spot + at + chips, chips)) * 2 + core)
 
     peers = [device(at) for at in range(1, chips)]
+    short = chips == 8
+
+    def inner(at):
+        z = chip_at(lax.rem(spot + at + chips, chips)) // 2
+        return (z == 1) | (z == 2)
+
+    facing = (3 - chip // 2) * 4 + lax.rem(chip, 2) * 2 + core
     place = {
+        "short": short, "inner": inner, "facing": facing,
+        "across": (group, me + 2 - 4 * lax.rem(chip, 2)),
         "peers": peers, "me": me, "core": core, "spot": spot, "side": side, "chips": chips, "chip_at": chip_at,
         "right": device(1), "left": device(-1),
         "near": (group, chip * 2 + 1 - core), "twin": (group + 1 - 2 * side, me),
     }
     local = [
         pltpu.make_async_copy(src, dst.at[me], local_sems.at[i])
-        for i, (src, dst) in enumerate(((up, u_all), (down, d_all), (weight, w_all)))
+        for i, (src, dst) in enumerate(((down, d_all), (weight, w_all)))
     ]
     for copy in local:
         copy.start()
+
+    slot = jnp.int32(0)
+    for t in range(owner.shape[0]):
+        slot = slot + jnp.where(tenant[0, 0] == t, owner[t], 0)
+    rank, width = down.shape
+    outputs = gradient.shape[1]
+    u_all[me, :, :outputs] = up[...]
+    u_all[me, :, outputs:] = jnp.broadcast_to(slot.astype(F32), (rank, 128)).astype(BF16)
 
     barrier = pltpu.get_barrier_semaphore()
     greeted = [*peers, place["near"], place["twin"]]
@@ -160,14 +192,20 @@
 
     sent = []
 
-    def pool(ref, to):
-        i = len(sent)
+    maybe = []
+
+    def pool(ref, to, only=None):
+        i = len(sent) + len(maybe)
         copy = pltpu.make_async_remote_copy(
             src_ref=ref, dst_ref=ref, send_sem=send_sems.at[i], recv_sem=recv_sems.at[i],
             device_id=to, device_id_type=MESH,
         )
-        copy.start()
-        sent.append(copy)
+        if only is None:
+            copy.start()
+            sent.append(copy)
+        else:
+            maybe.append((only, copy))
+            pl.when(only)(copy.start)
         return copy
 
     ups = Direct(place, pool, u_all)
@@ -177,18 +215,15 @@
     up_terms = Direct(place, pool, t_all)
 
     local[0].wait()
+    downs.begin()
     ups.begin()
     local[1].wait()
-    downs.begin()
-    local[2].wait()
     weights.begin()
+    downs.step(1)
     ups.pass_on()
     ups.settle()
 
-    rank, width = down.shape
-    outputs = gradient.shape[1]
     tile = 1024
-    slot = slot_ref[0]
     up_slot = u_all[slot][:, :outputs]
     back_low = (adapter_scale * dot(gradient[...], up_slot, (1, 1))).astype(BF16)
     back[...] = back_low
@@ -206,7 +241,6 @@
         out = pltpu.make_async_copy(stage, parts.at[me], local_sems.at[3])
         out.start()
         out.wait()
-    downs.step(1)
     terms.begin()
 
     def chunk(offset, which):
@@ -306,6 +340,8 @@
     )
     for copy in sent:
         copy.wait_send()
+    for only, copy in maybe:
+        pl.when(only)(copy.wait_send)
 
 
 def ring_order(chips):
@@ -331,17 +367,11 @@
     rows, width = hidden.shape
     outputs = output_gradient.shape[1]
     rank = adapter_down_maps.shape[2]
-    tenants = owner.shape[0]
     staged = n > 16
-    slot = jnp.sum(
-        jnp.where(token_block_tenant[0, 0] == jnp.arange(tenants, dtype=jnp.int32), owner, 0)
-    )
-    up = jnp.concatenate(
-        [adapter_up_maps[0], jnp.broadcast_to(slot.astype(BF16), (rank, 128))], axis=1
-    )
     down = adapter_down_maps[0].T
     count = 2 * copies_of(chips, True) + copies_of(chips, False) + 2 * (2 * chips - 1)
     vmem = pl.BlockSpec(memory_space=pltpu.VMEM)
+    smem = pl.BlockSpec(memory_space=pltpu.SMEM)
     hbm = pl.BlockSpec(memory_space=pl.ANY)
     out_shape = [
         jax.ShapeDtypeStruct((rows, outputs), BF16),
@@ -359,7 +389,7 @@
     scratch += [
         pltpu.VMEM((n,) + frozen_value_weight.shape, BF16),
         pltpu.VMEM((n, rank, width), BF16),
-        pltpu.VMEM((n,) + up.shape, BF16),
+        pltpu.VMEM((n, rank, outputs + 128), BF16),
         pltpu.VMEM((n, rank, outputs), BF16),
         pltpu.VMEM((rows, rank), BF16),
     ]
@@ -373,13 +403,16 @@
     results = pl.pallas_call(
         functools.partial(kernel, n, ring_order(chips), staged),
         out_shape=out_shape,
-        in_specs=[pl.BlockSpec(memory_space=pltpu.SMEM), vmem, vmem, hbm, hbm, hbm],
+        in_specs=[smem, smem, vmem, vmem, hbm, hbm, vmem],
         out_specs=out_specs,
         scratch_shapes=scratch,
         compiler_params=pltpu.CompilerParams(
             collective_id=0, has_side_effects=True, vmem_limit_bytes=56 << 20
         ),
-    )(slot.reshape(1), hidden, output_gradient, frozen_value_weight, down, up)
+    )(
+        owner, token_block_tenant, hidden, output_gradient, frozen_value_weight, down,
+        adapter_up_maps[0],
+    )
     values, grad_hidden, grad_down, grad_up = results[:4]
     return values, grad_hidden, grad_down.T[None], grad_up[None]
 

time: 123 us -> 118 us (0.959)
  local copies, waits for them, and re-layouts: 7.74 us -> 6.36 us
  other arithmetic: 1.29 us -> 0 us
    concatenate x1 -> x0, local copies, waits for them, and re-layouts: 1.38 us -> none  [per_device(): jnp.concatenate([adapter_up_maps[0], jnp.broadcast_to(slot.astype(BF16),...]
    reduce_sum x1 -> x0, other arithmetic: 1.29 us -> none  [per_device(): jnp.sum(jnp.where(token_block_tenant[0, 0] == jnp.arange(tenants, dtype=j...]
where the time goes in v4:
time: 118 us; the launch traced here: 117 us
  Pallas kernels  109 us (92%)
  local copies, waits for them, and re-layouts  6.36 us (5%)
  between operations  1.29 us (1%)
    pallas_call x1, Pallas kernels, per_device(): pl.pallas_call(functools.partial(kernel, n, ring_order(chips), staged), o...  109 us
    unnamed x8, local copies, waits for them, and re-layouts  6.36 us

profile of v4, /device:TPU:0, one launch (start us, length us, event | category | flops | bytes accessed | tf_op | source)
XLA Modules:
  0.0 117.0 jit_solution(17458937926615963948)
XLA Ops:
  1.3 109.3 %shard_map.102 = (bf16[128,512]{1,0:T(8,128)(2,1)}, bf16[128,8192]{1,0:T(8,128)(2,1)}, f32[32,8192]{1,0:T(8,128)}, f32[32,512]{1,0:T(8,128)}) custom-call(s32[16]{0:T(128)} %owner.1, s32[1,1]{1,0:T(1,128)S(6)} %copy.15.tenant, bf16[128,8192]{1,0:T(8,128)(2,1)} %hidden.1, bf16[128,512]{1,0:T(8,128)(2,1)} %gradient.1, bf16[512,512]{1,0:T(8,128)(2,1)} %weight.1, ...), custom_call_target="tpu_custom_call" | custom-call | tf_op jit(solution)/shard_map/pallas_call | solution.py:403
  110.6 1.6 %copy.16 = bf16[128,512]{1,0:T(8,128)(2,1)} copy(bf16[128,512]{1,0:T(8,128)(2,1)} %get-tuple-element.16) | data formatting | bytes 262144
  112.2 0.0 copy-start
  112.2 0.0 copy-start.1
  112.2 3.2 %copy.17 = bf16[128,8192]{1,0:T(8,128)(2,1)} copy(bf16[128,8192]{1,0:T(8,128)(2,1)} %get-tuple-element.17) | data formatting | bytes 4194304
  115.4 0.0 copy-done
  115.4 1.0 copy.18
  116.4 0.0 copy-done.1
  116.4 0.6 copy.19
Async XLA Ops:
  112.2 3.2 %copy-start = (f32[32,8192]{1,0:T(8,128)S(1)}, f32[32,8192]{1,0:T(8,128)}, u32[]{:S(2)}) copy-start(f32[32,8192]{1,0:T(8,128)} %get-tuple-element.10) | copy-start | bytes 3145732
  112.2 4.2 %copy-start.1 = (f32[32,512]{1,0:T(8,128)S(1)}, f32[32,512]{1,0:T(8,128)}, u32[]{:S(2)}) copy-start(f32[32,512]{1,0:T(8,128)} %get-tuple-element.11) | copy-start | bytes 196612

commit v5 on v4

--- a/solution.py
+++ b/solution.py
@@ -327,11 +327,19 @@
     terms.step(last)
     up_terms.pass_on()
     weights.cross(last - 1)
+    weights.settle(last - 1)
+    total = lax.fori_loop(0, 2, functools.partial(apply_weight, first=last - 1), total)
+    total = lax.fori_loop(0, 2, functools.partial(apply_weight, first=1 - last), total)
+    for k in (last - 1, last):
+        terms.settle(k)
+
+    @pl.loop(0, 6)
+    def _(i):
+        add_terms(i, last - 1)
+
     weights.cross(last)
-    for k in (last - 1, last):
-        weights.settle(k)
-        terms.settle(k)
-    total = use(total, last - 1, 3)
+    weights.settle(last)
+    total = lax.fori_loop(0, 2, functools.partial(apply_weight, first=last), total)
     values[...] = total.astype(BF16)
     up_terms.settle()
     grad_up[...] = lax.fori_loop(
@@ -342,6 +350,12 @@
         copy.wait_send()
     for only, copy in maybe:
         pl.when(only)(copy.wait_send)
+
+
+def copy_kernel(*refs):
+    half = len(refs) // 2
+    for source, target in zip(refs[:half], refs[half:]):
+        target[...] = source[...]
 
 
 def ring_order(chips):
@@ -413,7 +427,13 @@
         owner, token_block_tenant, hidden, output_gradient, frozen_value_weight, down,
         adapter_up_maps[0],
     )
-    values, grad_hidden, grad_down, grad_up = results[:4]
+    blocks = [
+        pl.BlockSpec((held.shape[0], held.shape[1] // 4), lambda i: (0, i))
+        for held in out_shape[:4]
+    ]
+    values, grad_hidden, grad_down, grad_up = pl.pallas_call(
+        copy_kernel, grid=(4,), out_shape=out_shape[:4], in_specs=blocks, out_specs=blocks
+    )(*results[:4])
     return values, grad_hidden, grad_down.T[None], grad_up[None]
 
 

time: 118 us -> 116 us (0.983)
  local copies, waits for them, and re-layouts: 6.36 us -> 0 us
  Pallas kernels: 109 us -> 115 us
    unnamed x8 -> x0, local copies, waits for them, and re-layouts: 6.36 us -> none
    pallas_call x0 -> x1, Pallas kernels: none -> 4.22 us  [per_device(): pl.pallas_call(copy_kernel, grid=(4,), out_shape=out_shape[:4], in_specs=...]
    pallas_call x1, Pallas kernels: 109 us -> 111 us  [per_device(): pl.pallas_call(functools.partial(kernel, n, ring_order(chips), staged), o...]
where the time goes in v5:
time: 116 us
  Pallas kernels  115 us (99%)
  between operations  1.29 us (1%)
    pallas_call x1, Pallas kernels, per_device(): pl.pallas_call(functools.partial(kernel, n, ring_order(chips), staged), o...  111 us
    pallas_call x1, Pallas kernels, per_device(): pl.pallas_call(copy_kernel, grid=(4,), out_shape=out_shape[:4], in_specs=...  4.22 us

profile of v5, /device:TPU:0, one launch (start us, length us, event | category | flops | bytes accessed | tf_op | source)
XLA Modules:
  0.0 116.2 jit_solution(695279404997216850)
XLA Ops:
  1.3 110.7 %shard_map.102 = (bf16[128,512]{1,0:T(8,128)(2,1)}, bf16[128,8192]{1,0:T(8,128)(2,1)}, f32[32,8192]{1,0:T(8,128)}, f32[32,512]{1,0:T(8,128)}) custom-call(s32[16]{0:T(128)} %owner.1, s32[1,1]{1,0:T(1,128)S(6)} %copy.11.tenant, bf16[128,8192]{1,0:T(8,128)(2,1)} %hidden.1, bf16[128,512]{1,0:T(8,128)(2,1)} %gradient.1, bf16[512,512]{1,0:T(8,128)(2,1)} %weight.1, ...), custom_call_target="tpu_custom_call" | custom-call | tf_op jit(solution)/shard_map/pallas_call | solution.py:417
  111.9 4.2 %shard_map.103 = (bf16[128,512]{1,0:T(8,128)(2,1)}, bf16[128,8192]{1,0:T(8,128)(2,1)}, f32[32,8192]{1,0:T(8,128)}, f32[32,512]{1,0:T(8,128)}) custom-call(bf16[128,512]{1,0:T(8,128)(2,1)} %get-tuple-element.12.refs_0_, bf16[128,8192]{1,0:T(8,128)(2,1)} %get-tuple-element.13.refs_1_, f32[32,8192]{1,0:T(8,128)} %get-tuple-element.14.refs_2_, ...), custom_call_target="tpu_custom_call" | custom-call | tf_op jit(solution)/shard_map/pallas_call | solution.py:434

commit v6 on v5

--- a/solution.py
+++ b/solution.py
@@ -250,25 +250,29 @@
         return (u_all[j][0:1, outputs:outputs + 1].astype(F32) == me.astype(F32)).astype(F32)
 
     def add_terms(i, first):
-        j = chunk(i // 2 + first, lax.rem(i, 2))
-        weight_of = share(j)
-        if staged:
-            get = pltpu.make_async_copy(parts.at[j], stage, local_sems.at[3])
-            get.start()
-            get.wait()
-
-        @pl.loop(0, width // tile)
-        def _(t):
-            at = pl.ds(pl.multiple_of(t * tile, tile), tile)
-            term = stage[:, at] if staged else parts[j, :, at]
-            grad_down[:, at] += weight_of * term.astype(F32)
+        pair = [chunk(i + first, 0), chunk(i + first, 1)]
+        for group in [[j] for j in pair] if staged else [pair]:
+            weights_of = [share(j) for j in group]
+            if staged:
+                get = pltpu.make_async_copy(parts.at[group[0]], stage, local_sems.at[3])
+                get.start()
+                get.wait()
+
+            @pl.loop(0, width // tile)
+            def _(t):
+                at = pl.ds(pl.multiple_of(t * tile, tile), tile)
+                total = grad_down[:, at]
+                for weight_of, j in zip(weights_of, group):
+                    term = stage[:, at] if staged else parts[j, :, at]
+                    total = total + weight_of * term.astype(F32)
+                grad_down[:, at] = total
 
     rows = w_all.shape[1]
 
     def apply_weight(i, total, first):
-        j = chunk(i // 2 + first, lax.rem(i, 2))
-        at = pl.ds(pl.multiple_of(j * rows, 128), rows)
-        block = w_all[j]
+        j = chunk(i + first, 0)
+        at = pl.ds(pl.multiple_of(j * rows, 128), 2 * rows)
+        block = w_all[pl.ds(j, 2)].reshape(2 * rows, outputs)
         base = dot(gradient[...], block, (1, 1))
         grad_hidden[:, at] = (base + grad_hidden[:, at].astype(F32)).astype(BF16)
         return total + dot(hidden[:, at], block, (1, 0))
@@ -304,10 +308,10 @@
 
     def use(total, first, offsets):
         total = lax.fori_loop(
-            0, 2 * offsets, functools.partial(apply_weight, first=first), total
+            0, offsets, functools.partial(apply_weight, first=first), total
         )
 
-        @pl.loop(0, 2 * offsets)
+        @pl.loop(0, offsets)
         def _(i):
             add_terms(i, first)
 
@@ -328,18 +332,18 @@
     up_terms.pass_on()
     weights.cross(last - 1)
     weights.settle(last - 1)
-    total = lax.fori_loop(0, 2, functools.partial(apply_weight, first=last - 1), total)
-    total = lax.fori_loop(0, 2, functools.partial(apply_weight, first=1 - last), total)
+    total = lax.fori_loop(0, 1, functools.partial(apply_weight, first=last - 1), total)
+    total = lax.fori_loop(0, 1, functools.partial(apply_weight, first=1 - last), total)
     for k in (last - 1, last):
         terms.settle(k)
 
-    @pl.loop(0, 6)
+    @pl.loop(0, 3)
     def _(i):
         add_terms(i, last - 1)
 
     weights.cross(last)
     weights.settle(last)
-    total = lax.fori_loop(0, 2, functools.partial(apply_weight, first=last), total)
+    total = lax.fori_loop(0, 1, functools.partial(apply_weight, first=last), total)
     values[...] = total.astype(BF16)
     up_terms.settle()
     grad_up[...] = lax.fori_loop(

time: 116 us -> 114 us (0.983)
  Pallas kernels: 115 us -> 113 us
    pallas_call x1, Pallas kernels: 111 us -> 109 us  [per_device(): pl.pallas_call(functools.partial(kernel, n, ring_order(chips), staged), o...]
where the time goes in v6:
time: 114 us
  Pallas kernels  113 us (99%)
  between operations  1.29 us (1%)
    pallas_call x1, Pallas kernels, per_device(): pl.pallas_call(functools.partial(kernel, n, ring_order(chips), staged), o...  109 us
    pallas_call x1, Pallas kernels, per_device(): pl.pallas_call(copy_kernel, grid=(4,), out_shape=out_shape[:4], in_specs=...  4.22 us

profile of v6, /device:TPU:0, one launch (start us, length us, event | category | flops | bytes accessed | tf_op | source)
XLA Modules:
  0.0 114.2 jit_solution(16328854770013793364)
XLA Ops:
  1.3 108.7 %shard_map.102 = (bf16[128,512]{1,0:T(8,128)(2,1)}, bf16[128,8192]{1,0:T(8,128)(2,1)}, f32[32,8192]{1,0:T(8,128)}, f32[32,512]{1,0:T(8,128)}) custom-call(s32[16]{0:T(128)} %owner.1, s32[1,1]{1,0:T(1,128)S(6)} %copy.11.tenant, bf16[128,8192]{1,0:T(8,128)(2,1)} %hidden.1, bf16[128,512]{1,0:T(8,128)(2,1)} %gradient.1, bf16[512,512]{1,0:T(8,128)(2,1)} %weight.1, ...), custom_call_target="tpu_custom_call" | custom-call | tf_op jit(solution)/shard_map/pallas_call | solution.py:421
  109.9 4.2 %shard_map.103 = (bf16[128,512]{1,0:T(8,128)(2,1)}, bf16[128,8192]{1,0:T(8,128)(2,1)}, f32[32,8192]{1,0:T(8,128)}, f32[32,512]{1,0:T(8,128)}) custom-call(bf16[128,512]{1,0:T(8,128)(2,1)} %get-tuple-element.12.refs_0_, bf16[128,8192]{1,0:T(8,128)(2,1)} %get-tuple-element.13.refs_1_, f32[32,8192]{1,0:T(8,128)} %get-tuple-element.14.refs_2_, ...), custom_call_target="tpu_custom_call" | custom-call | tf_op jit(solution)/shard_map/pallas_call | solution.py:438
